TPU v7x, 32 devices: a whole 2x2x4 slice. The times are simulated.
32 devices in a mesh: dp: 16 (over z, y, core), tensor: 2 (over x).
Axes of the slice: x: 2, y: 2, z: 4, core: 2. Of those that a mesh axis runs over, the one named last changes fastest.
Arguments:
- context: bfloat16 [4096, 3072], P('dp', 'tensor'), may hold values from -6 to 6
- residual: bfloat16 [4096, 5120], P(('dp', 'tensor')), may hold values from -36 to 36
- out_weight: bfloat16 [5120, 3072], P('dp', 'tensor'), may hold values from -0.109375 to 0.109375
- norm_gain: float32 [5120], replicated, may hold values from 0.5 to 2
- normed_grad: bfloat16 [4096, 5120], P(('dp', 'tensor')), may hold values from -6 to 6
- stream_grad: bfloat16 [4096, 5120], P(('dp', 'tensor')), may hold values from -6 to 6
- sketch_in: int32 [3072, 64], P('tensor'), may hold values from -1 to 1
- sketch_out: int32 [5120, 64], replicated, may hold values from -1 to 1
- example_ids: int32 [4096], P(('dp', 'tensor')), may hold values from 0 to 15, as said below
Outputs:
- grad_hidden: bfloat16 [4096, 5120], P(('dp', 'tensor'))
- grad_context: bfloat16 [4096, 3072], P('dp', 'tensor')
- sketches: float32 [16, 4096], P('dp', 'tensor')
Inputs may be any that keep to these rules, and one draw needn't show every extreme that they name: `example_ids`: each aligned block of 256 tokens belongs to one example, and every example owns exactly one such block.
All inputs are finite; a program needn't handle non-finite values.
Results may differ from a plain program's by a relative error of at most 0.0095.
Values may be sent and summed in bfloat16 or wider, within the bound.
A program may use at most 128 MiB of HBM per device.

v0:
```python
import math

import jax
import jax.numpy as jnp
from jax import lax
from jax.sharding import PartitionSpec as P

epsilon = 1e-06


def on_device(
    context,
    residual,
    out_weight,
    norm_gain,
    normed_grad,
    stream_grad,
    sketch_in,
    sketch_out,
    example_ids,
):
    tensor_count = lax.axis_size("tensor")
    example_count = lax.axis_size("dp")
    width = residual.shape[1]
    local_heads = context.shape[1]
    token_count = context.shape[0]
    row_count = residual.shape[0]
    sketch_rank = sketch_in.shape[1]
    in_scale = 1.0 / math.sqrt(local_heads * tensor_count)
    out_scale = 1.0 / math.sqrt(width)
    in_table = sketch_in.astype(jnp.bfloat16)
    weight_full = lax.all_gather(out_weight, "dp", axis=0, tiled=True)
    summed = lax.psum_scatter(
        lax.dot_general(
            context, weight_full, (((1,), (1,)), ((), ())), preferred_element_type=jnp.float32
        ).astype(jnp.bfloat16),
        "tensor",
        scatter_dimension=0,
        tiled=True,
    ).astype(jnp.float32)
    projected_all = jnp.dot(context, in_table, preferred_element_type=jnp.float32) * in_scale
    in_proj = lax.psum_scatter(
        projected_all.astype(jnp.bfloat16), "tensor", scatter_dimension=0, tiled=True
    ).astype(jnp.float32)
    hidden = residual.astype(jnp.float32) + summed
    rstd = lax.rsqrt(jnp.mean(hidden * hidden, axis=-1, keepdims=True) + epsilon)
    weighted = norm_gain[None, :] * normed_grad.astype(jnp.float32)
    inner = jnp.mean(weighted * hidden, axis=-1, keepdims=True)
    grad_hidden = (
        stream_grad.astype(jnp.float32) + rstd * weighted - hidden * (rstd * rstd * rstd) * inner
    ).astype(jnp.bfloat16)
    grad_all = lax.all_gather(grad_hidden, "tensor", axis=0, tiled=True)
    grad_full = jnp.dot(
        grad_all,
        lax.all_gather(out_weight, "dp", axis=0, tiled=True),
        preferred_element_type=jnp.float32,
    )
    grad_context = grad_full.astype(jnp.bfloat16)
    out_proj = (
        jnp.dot(grad_hidden, sketch_out.astype(jnp.bfloat16), preferred_element_type=jnp.float32)
        * out_scale
    )
    pairs = (in_proj[:, :, None] * out_proj[:, None, :]).reshape(
        row_count, sketch_rank * sketch_rank
    )
    one_hot = (example_ids[:, None] == jnp.arange(example_count, dtype=jnp.int32)[None, :]).astype(
        jnp.float32
    )
    partial_sketch = lax.dot_general(
        one_hot,
        pairs,
        (((0,), (0,)), ((), ())),
        precision=lax.Precision.HIGHEST,
        preferred_element_type=jnp.float32,
    )
    tensor_summed = lax.psum_scatter(
        partial_sketch.astype(jnp.bfloat16), "tensor", scatter_dimension=1, tiled=True
    ).astype(jnp.float32)
    local_sketch = lax.psum_scatter(tensor_summed, "dp", scatter_dimension=0, tiled=True)
    sketches = local_sketch * (1.0 / math.sqrt(token_count))
    return (grad_hidden, grad_context, sketches)


def solution(mesh):
    return jax.shard_map(
        on_device,
        mesh=mesh,
        in_specs=(
            P("dp", "tensor"),
            P(("dp", "tensor"), None),
            P("dp", "tensor"),
            P(),
            P(("dp", "tensor"), None),
            P(("dp", "tensor"), None),
            P("tensor", None),
            P(),
            P(("dp", "tensor")),
        ),
        out_specs=(P(("dp", "tensor"), None), P("dp", "tensor"), P("dp", "tensor")),
        check_vma=False,
    )
```

profile of v0, /device:TPU:0, one launch (start us, length us, event | category | flops | bytes accessed | tf_op | source)
XLA Modules:
  0.0 288.0 jit_solution(6218070786134259774)
XLA Ops:
  8.0 0.0 copy-start
  8.0 0.0 all-gather.3.cloned.1.call-start
  8.1 0.7 all-gather.3.cloned.1.call-update
  8.7 0.0 reduce-scatter.10.cloned.1.call-start
  8.8 0.3 copy-done
  9.1 1.3 fusion
  10.5 0.7 copy.14
  11.2 0.0 reduce-scatter.10.cloned.1.call-update
  11.2 0.0 reduce-scatter.6.cloned.1.call-start
  11.3 122.9 %all-gather.3.cloned.1.call-done = bf16[5120,1536]{1,0:T(8,128)(2,1)} async-done(((bf16[320,1536]{1,0:T(8,128)(2,1)}), bf16[5120,1536]{1,0:T(8,128)(2,1)}) %all-gather.3.cloned.1.call-update) | async-done | bytes 15728656 | tf_op jit(solution)/shard_map/all_gather | solution.py:32
  134.2 16.9 %convolution_convert_fusion = bf16[256,5120]{1,0:T(8,128)(2,1)} fusion(bf16[256,1536]{1,0:T(8,128)(2,1)S(1)} %copy-done, bf16[5120,1536]{1,0:T(8,128)(2,1)} %all-gather.3.cloned.1.call-done), kind=kOutput, calls=%fused_computation | convolution fusion | flops 4027842560 | bytes 19136512 | tf_op jit(solution)/shard_map/dot_general | solution.py:34
  151.1 0.0 copy-start.2
  151.1 0.0 copy-start.3
  151.1 0.0 copy-start.7
  151.1 0.0 reduce-scatter.6.cloned.1.call-update
  151.1 0.0 reduce-scatter.8.cloned.1.call-start
  151.1 0.0 reduce-scatter.10.cloned.1.call-done
  151.2 1.0 copy.15
  152.2 34.7 %reduce-scatter.6.cloned.1.call-done = bf16[128,5120]{1,0:T(8,128)(2,1)} async-done(((bf16[256,5120]{1,0:T(8,128)(2,1)}), bf16[128,5120]{1,0:T(8,128)(2,1)}) %reduce-scatter.6.cloned.1.call-update) | async-done | bytes 1310736 | tf_op jit(solution)/shard_map/reduce_scatter | solution.py:33
  186.9 0.0 copy-done.2
  186.9 0.0 copy-done.3
  186.9 0.0 copy-done.7
  186.9 0.0 copy-start.4
  186.9 0.0 copy-start.5
  186.9 0.0 copy-start.6
  186.9 2.4 multiply_reduce_fusion.1
  189.3 0.0 copy-done.4
  189.3 0.0 copy-done.5
  189.3 0.1 copy-done.6
  189.4 1.4 subtract_convert_fusion
  190.7 0.0 copy-start.1
  190.8 0.0 copy-start.8
  190.8 2.4 convolution_multiply_fusion.1
  193.1 0.0 copy-start.9
  193.2 0.3 broadcast_multiply_fusion
  193.4 0.0 copy-done.8
  193.4 1.8 convolution_convert_fusion.1
  195.2 0.0 copy-done.1
  195.2 0.0 reduce-scatter.8.cloned.1.call-update
  195.2 0.0 all-gather.5.cloned.1.call-start
  195.3 0.7 all-gather.5.cloned.1.call-update
  196.0 0.0 copy-done.9
  196.0 0.6 dynamic-slice
  196.6 9.0 %reduce-scatter.8.cloned.1.call-done = bf16[16,2048]{1,0:T(8,128)(2,1)} async-done(((bf16[16,4096]{1,0:T(8,128)(2,1)}), bf16[16,2048]{1,0:T(8,128)(2,1)}) %reduce-scatter.8.cloned.1.call-update) | async-done | bytes 65552 | tf_op jit(solution)/shard_map/reduce_scatter | solution.py:76
  205.5 62.3 %all-reduce.2 = f32[16,2048]{1,0:T(8,128)S(1)} all-reduce(bf16[16,2048]{1,0:T(8,128)(2,1)} %reduce-scatter.8.cloned.1.call-done), channel_id=5, replica_groups=mesh['dp'=16,'tensor'=2] {'dp'}, use_global_device_ids=true, to_apply=%region_5.0.clone | all-reduce | flops 32768 | bytes 196608
  267.8 1.2 dynamic-slice_multiply_fusion
  269.0 0.0 all-gather.5.cloned.1.call-done
  269.0 11.4 %convolution_convert_fusion.2 = bf16[256,1536]{1,0:T(8,128)(2,1)} fusion(bf16[256,5120]{1,0:T(8,128)(2,1)} %all-gather.5.cloned.1.call-done, bf16[5120,1536]{1,0:T(8,128)(2,1)} %all-gather.3.cloned.1.call-done), kind=kOutput, calls=%fused_computation.7 | convolution fusion | flops 4026925056 | bytes 19136512 | tf_op jit(solution)/shard_map/dot_general | solution.py:53
  (2 shorter events, 0.0 us)
Async XLA Ops:
  8.0 1.1 copy-start
  8.0 126.2 %all-gather.3.cloned.1.call-start = ((), (), s32[]{:S(2)}) async-start(), calls=%async_computation.3 | async-start | bytes 16711680 | tf_op jit(solution)/shard_map/all_gather | solution.py:32
  8.7 142.4 %reduce-scatter.10.cloned.1.call-start = ((), (), s32[]{:S(2)}) async-start(), calls=%async_computation.7 | async-start | bytes 98304
  11.2 175.6 %reduce-scatter.6.cloned.1.call-start = ((), (), s32[]{:S(2)}) async-start(), calls=%async_computation.4 | async-start | bytes 3932160 | tf_op jit(solution)/shard_map/reduce_scatter | solution.py:33
  151.1 35.8 %copy-start.2 = (bf16[128,5120]{1,0:T(8,128)(2,1)S(1)}, bf16[128,5120]{1,0:T(8,128)(2,1)}, u32[]{:S(2)}) copy-start(bf16[128,5120]{1,0:T(8,128)(2,1)} %param.13) | copy-start | bytes 3932164
  151.1 35.8 %copy-start.3 = (bf16[128,5120]{1,0:T(8,128)(2,1)S(1)}, bf16[128,5120]{1,0:T(8,128)(2,1)}, u32[]{:S(2)}) copy-start(bf16[128,5120]{1,0:T(8,128)(2,1)} %param.10) | copy-start | bytes 3932164
  151.1 35.8 %copy-start.7 = (f32[5120]{0:T(1024)S(1)}, f32[5120]{0:T(1024)}, u32[]{:S(2)}) copy-start(f32[5120]{0:T(1024)} %param.12) | copy-start | bytes 61444
  151.1 54.4 %reduce-scatter.8.cloned.1.call-start = ((), (), s32[]{:S(2)}) async-start(), calls=%async_computation.6 | async-start | bytes 196608 | tf_op jit(solution)/shard_map/reduce_scatter | solution.py:76
  186.9 2.4 copy-start.4
  186.9 2.4 copy-start.5
  186.9 2.5 copy-start.6
  190.7 4.5 %copy-start.1 = (bf16[128,5120]{1,0:T(8,128)(2,1)}, bf16[128,5120]{1,0:T(8,128)(2,1)S(1)}, u32[]{:S(2)}) copy-start(bf16[128,5120]{1,0:T(8,128)(2,1)S(1)} %subtract_convert_fusion) | copy-start | bytes 3932164
  190.8 2.7 copy-start.8
  193.1 2.8 copy-start.9
  195.2 73.8 %all-gather.5.cloned.1.call-start = ((), (), s32[]{:S(2)}) async-start(), calls=%async_computation.5 | async-start | bytes 3932160 | tf_op jit(solution)/shard_map/all_gather | solution.py:52
Sparse Core Ops, SparseCore 0:
  11.1 122.9 all-gather.2
Sparse Core Ops, SparseCore 1:
  12.0 12.5 reduce-scatter.9
  151.2 35.6 reduce-scatter.5
  195.3 10.2 reduce-scatter.7
  207.7 38.8 all-gather.4
where the time goes:
time: 288 us
  waiting for transfers between devices  168 us (58%)
  blocking collectives  62.3 us (22%)
  matrix products  33.7 us (12%)
  between operations  15.8 us (5%)
  other arithmetic  5.17 us (2%)
    all_gather x1, waiting for transfers between devices, on_device(): weight_full = lax.all_gather(out_weight, 'dp', axis=0, tiled=True)  123 us
    unnamed x1, blocking collectives  62.3 us
    reduce_scatter x1, waiting for transfers between devices, on_device(): lax.psum_scatter(lax.dot_general(context, weight_full, (((1,), (1,)), (()...  34.7 us
    dot_general x1, matrix products, on_device(): lax.dot_general(context, weight_full, (((1,), (1,)), ((), ())), preferred...  16.9 us
    dot_general x1, matrix products, on_device(): jnp.dot(grad_all, lax.all_gather(out_weight, 'dp', axis=0, tiled=True), p...  11.4 us
    reduce_scatter x1, waiting for transfers between devices, on_device(): lax.psum_scatter(partial_sketch.astype(jnp.bfloat16), 'tensor', scatter_d...  8.95 us
  transfers between devices with their start and end apart: 5, of which 3 were waited for; matrix products, arithmetic and copies ran while one was open for 8% of the time, Pallas kernels for 0%

commit v1 on v0

v1 whole, which is shorter than its diff:
```python
import functools
import math

import jax
import jax.numpy as jnp
from jax import lax
from jax.experimental import pallas as pl
from jax.experimental.pallas import tpu as pltpu
from jax.sharding import PartitionSpec as P

epsilon = 1e-06
MESH = pl.DeviceIdType.MESH
f32 = jnp.float32
bf16 = jnp.bfloat16


def kernel(
    dp,
    tp,
    group,
    context_hbm,
    residual_hbm,
    weight_hbm,
    gain_ref,
    normed_hbm,
    stream_hbm,
    in_hbm,
    out_hbm,
    ids_ref,
    gh_out,
    gc_out,
    sk_out,
    weight,
    context,
    residual,
    normed,
    stream,
    in_table,
    out_table,
    part_all,
    part_in,
    hidden,
    square,
    cross,
    gh_all,
    total,
    proj_all,
    proj_in,
    sk_all,
    sk_tensor,
    sk_send,
    sk_in,
    load_sem,
    w_send,
    w_recv,
    part_send,
    part_recv,
    gh_send,
    gh_recv,
    proj_send,
    proj_recv,
    skt_send,
    skt_recv,
    skd_send,
    skd_recv,
):
    me = lax.axis_index("dp")
    t = lax.axis_index("tensor")
    lines = dp // 4
    a, b, c = me // 4, lax.rem(me // 2, 2), lax.rem(me, 2)
    rows = residual.shape[0]
    width = residual.shape[1]
    shard = weight_hbm.shape[0]
    cols = group * shard
    groups = width // cols
    in_scale = 1.0 / math.sqrt(context.shape[1] * tp)
    out_scale = 1.0 / math.sqrt(width)

    def load(k, source, target):
        return pltpu.make_async_copy(source, target, load_sem.at[k])

    def place(i):
        return pl.ds(pl.multiple_of(i * shard, shard), shard)

    def block(g):
        return pl.ds(pl.multiple_of(g * cols, cols), cols)

    loads = [
        load(0, weight_hbm, weight.at[place(me)]),
        load(1, context_hbm, context),
        load(2, in_hbm, in_table),
        load(3, residual_hbm, residual),
        load(4, normed_hbm, normed),
        load(5, stream_hbm, stream),
        load(6, out_hbm, out_table),
    ]
    for copy in loads:
        copy.start()

    barrier = pltpu.get_barrier_semaphore()

    @pl.loop(1, dp)
    def _(k):
        pl.semaphore_signal(
            barrier, inc=1, device_id=(lax.rem(me + k, dp), t), device_id_type=MESH
        )

    for k in range(1, tp):
        pl.semaphore_signal(
            barrier, inc=1, device_id=(me, lax.rem(t + k, tp)), device_id_type=MESH
        )
    pl.semaphore_wait(barrier, dp - 1 + tp - 1)

    def index(a0, b0, c0):
        return (a0 * 2 + b0) * 2 + c0

    def send_weight(i, way, to):
        return pltpu.make_async_remote_copy(
            src_ref=weight.at[place(i)],
            dst_ref=weight.at[place(i)],
            send_sem=w_send.at[way, i],
            recv_sem=w_recv.at[i],
            device_id=(to, t),
            device_id_type=MESH,
        )

    def await_weight(i):
        send_weight(i, 0, index(a, b, 1 - c)).wait_recv()

    def peer(k):
        return lax.rem(t + 1 + k, tp)

    def ways(a0, act):
        i = index(a0, b, c)

        @pl.when((a0 >= a) & (a > 0))
        def _():
            act(send_weight(i, 2, index(a - 1, b, c)))

        @pl.when((a0 <= a) & (a < lines - 1))
        def _():
            act(send_weight(i, 3, index(a + 1, b, c)))

        act(send_weight(i, 1, index(a, 1 - b, c)))
        act(send_weight(i, 0, index(a, b, 1 - c)))

    def pass_on(a0, column):
        @pl.when(column == 0)
        def _():
            @pl.when(a0 != a)
            def _():
                await_weight(index(a0, b, c))

            ways(a0, lambda copy: copy.start())

        @pl.when(column == 1)
        def _():
            i = index(a0, 1 - b, c)
            await_weight(i)
            send_weight(i, 0, index(a, b, 1 - c)).start()

    def send_part(k, g):
        return pltpu.make_async_remote_copy(
            src_ref=part_all.at[g, pl.ds(pl.multiple_of(peer(k) * rows, rows), rows)],
            dst_ref=part_in.at[tp - 2 - k, g],
            send_sem=part_send.at[k, g],
            recv_sem=part_recv.at[tp - 2 - k, g],
            device_id=(me, peer(k)),
            device_id_type=MESH,
        )

    def await_part(k, g):
        pltpu.make_async_remote_copy(
            src_ref=part_in.at[k, g],
            dst_ref=part_in.at[k, g],
            send_sem=part_send.at[k, g],
            recv_sem=part_recv.at[k, g],
            device_id=(me, peer(k)),
            device_id_type=MESH,
        ).wait_recv()

    def forward(g):
        part_all[g] = lax.dot_general(
            context[...],
            weight[block(g), :],
            (((1,), (1,)), ((), ())),
            preferred_element_type=f32,
        ).astype(bf16)
        for k in range(tp - 1):
            send_part(k, g).start()

    own_rows = pl.ds(pl.multiple_of(t * rows, rows), rows)

    def weighted_of(g):
        return gain_ref[:, block(g)] * normed[:, block(g)].astype(f32)

    def gather_stats(g):
        value = residual[:, block(g)].astype(f32) + part_all[g, own_rows, :].astype(f32)
        for k in range(tp - 1):
            await_part(k, g)
            value = value + part_in[k, g].astype(f32)
        hidden[g] = value
        square[...] += jnp.sum(value * value, axis=-1, keepdims=True)
        cross[...] += jnp.sum(value * weighted_of(g), axis=-1, keepdims=True)

    square[...] = jnp.zeros_like(square)
    cross[...] = jnp.zeros_like(cross)
    loads[0].wait()

    def send_proj(k):
        return pltpu.make_async_remote_copy(
            src_ref=proj_all.at[pl.ds(pl.multiple_of(peer(k) * rows, rows), rows)],
            dst_ref=proj_in.at[tp - 2 - k],
            send_sem=proj_send.at[k],
            recv_sem=proj_recv.at[tp - 2 - k],
            device_id=(me, peer(k)),
            device_id_type=MESH,
        )

    def event(e, distance, act):
        side, column = lax.rem(e, 2), e // 2
        a0 = a + (2 * side - 1) * (distance - column)
        there = (distance - column >= 0) & (a0 >= 0) & (a0 < lines)

        @pl.when(there & ((distance != column) | (side == 0)))
        def _():
            act(a0, column)

    def whole_chip(a0, column):
        b0 = lax.rem(b + column, 2)
        await_weight(index(a0, b0, 1 - c))

    def chip_forward(a0, column):
        whole_chip(a0, column)
        forward(a0 * 2 + lax.rem(b + column, 2))

    def chip_stats(a0, column):
        gather_stats(a0 * 2 + lax.rem(b + column, 2))

    def first_loads():
        loads[1].wait()
        loads[2].wait()
        proj_all[...] = (
            jnp.dot(context[...], in_table[...].astype(f32).astype(bf16), preferred_element_type=f32)
            * in_scale
        ).astype(bf16)
        for k in range(tp - 1):
            send_proj(k).start()
        for copy in loads[3:]:
            copy.wait()

    pass_on(a, jnp.int32(0))
    first_loads()

    @pl.loop(1, lines + 3)
    def _(s):
        @pl.loop(0, 4)
        def _(e):
            event(e, s, pass_on)

        if group == 2:

            @pl.loop(0, 4)
            def _(e):
                event(e, s - 1, chip_forward)

            @pl.loop(0, 4)
            def _(e):
                event(e, s - 2, chip_stats)

        else:

            @pl.loop(0, 4)
            def _(e):
                event(e, s - 1, whole_chip)

    if group != 2:

        @pl.loop(0, groups)
        def _(g):
            forward(g)

        @pl.loop(0, groups)
        def _(g):
            gather_stats(g)

    rstd = lax.rsqrt(square[...] * (1.0 / width) + epsilon)
    pull = rstd * rstd * rstd * (cross[...] * (1.0 / width))
    square[...] = rstd
    cross[...] = pull

    def send_gh(k, g):
        return pltpu.make_async_remote_copy(
            src_ref=gh_all.at[t, g],
            dst_ref=gh_all.at[t, g],
            send_sem=gh_send.at[k, g],
            recv_sem=gh_recv.at[tp - 2 - k, g],
            device_id=(me, peer(k)),
            device_id_type=MESH,
        )

    def await_gh(k, g):
        pltpu.make_async_remote_copy(
            src_ref=gh_all.at[peer(k), g],
            dst_ref=gh_all.at[peer(k), g],
            send_sem=gh_send.at[k, g],
            recv_sem=gh_recv.at[k, g],
            device_id=(me, peer(k)),
            device_id_type=MESH,
        ).wait_recv()

    @pl.loop(0, groups)
    def _(g):
        value = (
            stream[:, block(g)].astype(f32)
            + square[...] * weighted_of(g)
            - hidden[g] * cross[...]
        ).astype(bf16)
        gh_all[t, g] = value
        gh_out[:, block(g)] = value
        for k in range(tp - 1):
            send_gh(k, g).start()

    out_proj = (
        jnp.dot(gh_out[...], out_table[...].astype(f32).astype(bf16), preferred_element_type=f32)
        * out_scale
    )
    in_proj = proj_all[own_rows, :].astype(f32)
    for k in range(tp - 1):
        send_proj(k).wait_recv()
    for k in range(tp - 1):
        in_proj = in_proj + proj_in[k].astype(f32)
    sk_all[...] = lax.dot_general(
        in_proj,
        out_proj,
        (((0,), (0,)), ((), ())),
        precision=lax.Precision.HIGHEST,
        preferred_element_type=f32,
    )
    piece = sk_out.shape[0]

    def send_skt(k):
        return pltpu.make_async_remote_copy(
            src_ref=sk_all.at[pl.ds(pl.multiple_of(peer(k) * piece, piece), piece)],
            dst_ref=sk_tensor.at[tp - 2 - k],
            send_sem=skt_send.at[k],
            recv_sem=skt_recv.at[tp - 2 - k],
            device_id=(me, peer(k)),
            device_id_type=MESH,
        )

    for k in range(tp - 1):
        send_skt(k).start()

    def backward(row, g0):
        @pl.loop(0, groups)
        def _(g):
            g0(g)
            product = jnp.dot(gh_all[row, g], weight[block(g), :], preferred_element_type=f32)

            @pl.when(g == 0)
            def _():
                total[...] = product

            @pl.when(g > 0)
            def _():
                total[...] += product

        gc_out[pl.ds(pl.multiple_of(row * rows, rows), rows), :] = total[...].astype(bf16)

    backward(t, lambda g: None)

    summed = sk_all[pl.ds(pl.multiple_of(t * piece, piece), piece), :]
    for k in range(tp - 1):
        send_skt(k).wait_recv()
    for k in range(tp - 1):
        summed = summed + sk_tensor[k]
    summed = summed * (1.0 / math.sqrt(context.shape[0]))
    sk_out[...] = summed

    def send_skd(r):
        return pltpu.make_async_remote_copy(
            src_ref=sk_send.at[r],
            dst_ref=sk_in.at[me],
            send_sem=skd_send.at[r],
            recv_sem=skd_recv.at[me],
            device_id=(r, t),
            device_id_type=MESH,
        )

    def await_skd(r):
        pltpu.make_async_remote_copy(
            src_ref=sk_in.at[r],
            dst_ref=sk_in.at[r],
            send_sem=skd_send.at[r],
            recv_sem=skd_recv.at[r],
            device_id=(r, t),
            device_id_type=MESH,
        ).wait_recv()

    owner = jnp.broadcast_to(ids_ref[0:1, 0:1], sk_out.shape)

    @pl.loop(1, dp)
    def _(k):
        r = lax.rem(me + k, dp)
        sk_send[r] = jnp.where(owner == r, sk_out[...], 0.0)
        send_skd(r).start()

    for k in range(tp - 1):
        backward(peer(k), functools.partial(await_gh, k))

    sk_out[...] = jnp.where(owner == me, sk_out[...], 0.0)

    @pl.loop(1, dp)
    def _(k):
        r = lax.rem(me + k, dp)
        await_skd(r)
        sk_out[...] += sk_in[r]

    @pl.loop(0, lines)
    def _(a0):
        ways(a0, lambda copy: copy.wait_send())
        i = index(a0, 1 - b, c)
        send_weight(i, 0, index(a, b, 1 - c)).wait_send()

    for k in range(tp - 1):
        send_proj(k).wait_send()
        send_skt(k).wait_send()

        @pl.loop(0, groups)
        def _(g):
            send_part(k, g).wait_send()
            send_gh(k, g).wait_send()

    @pl.loop(1, dp)
    def _(k):
        send_skd(lax.rem(me + k, dp)).wait_send()


def on_device(
    context,
    residual,
    out_weight,
    norm_gain,
    normed_grad,
    stream_grad,
    sketch_in,
    sketch_out,
    example_ids,
):
    tp = lax.axis_size("tensor")
    dp = lax.axis_size("dp")
    tokens, heads = context.shape
    rows, width = residual.shape
    shard = out_weight.shape[0]
    rank = sketch_in.shape[1]
    group = 2
    while (group * shard) % 128:
        group *= 2
    cols = group * shard
    groups = width // cols
    piece = rank // tp
    hbm = pl.BlockSpec(memory_space=pl.ANY)
    vmem = pl.BlockSpec(memory_space=pltpu.VMEM)
    dma = pltpu.SemaphoreType.DMA
    flops = 4 * tokens * heads * width
    grad_hidden, grad_context, sketch = pl.pallas_call(
        functools.partial(kernel, dp, tp, group),
        out_shape=(
            jax.ShapeDtypeStruct((rows, width), bf16),
            jax.ShapeDtypeStruct((tokens, heads), bf16),
            jax.ShapeDtypeStruct((piece, rank), f32),
        ),
        in_specs=[hbm, hbm, hbm, vmem, hbm, hbm, hbm, hbm, vmem],
        out_specs=(vmem, vmem, vmem),
        scratch_shapes=[
            pltpu.VMEM((width, heads), bf16),
            pltpu.VMEM((tokens, heads), bf16),
            pltpu.VMEM((rows, width), bf16),
            pltpu.VMEM((rows, width), bf16),
            pltpu.VMEM((rows, width), bf16),
            pltpu.VMEM((heads, rank), jnp.int32),
            pltpu.VMEM((width, rank), jnp.int32),
            pltpu.VMEM((groups, tokens, cols), bf16),
            pltpu.VMEM((tp - 1, groups, rows, cols), bf16),
            pltpu.VMEM((groups, rows, cols), f32),
            pltpu.VMEM((rows, 1), f32),
            pltpu.VMEM((rows, 1), f32),
            pltpu.VMEM((tp, groups, rows, cols), bf16),
            pltpu.VMEM((rows, heads), f32),
            pltpu.VMEM((tokens, rank), bf16),
            pltpu.VMEM((tp - 1, rows, rank), bf16),
            pltpu.VMEM((rank, rank), f32),
            pltpu.VMEM((tp - 1, piece, rank), f32),
            pltpu.VMEM((dp, piece, rank), f32),
            pltpu.VMEM((dp, piece, rank), f32),
            dma((7,)),
            dma((4, dp)),
            dma((dp,)),
            dma((tp - 1, groups)),
            dma((tp - 1, groups)),
            dma((tp - 1, groups)),
            dma((tp - 1, groups)),
            dma((tp - 1,)),
            dma((tp - 1,)),
            dma((tp - 1,)),
            dma((tp - 1,)),
            dma((dp,)),
            dma((dp,)),
        ],
        compiler_params=pltpu.CompilerParams(
            collective_id=0, has_side_effects=True, vmem_limit_bytes=56 * 1024 * 1024
        ),
        cost_estimate=pl.CostEstimate(
            flops=flops, bytes_accessed=16 * 1024 * 1024, transcendentals=0
        ),
    )(
        context,
        residual,
        out_weight,
        norm_gain.reshape(1, width),
        normed_grad,
        stream_grad,
        sketch_in,
        sketch_out,
        example_ids.reshape(1, rows),
    )
    return (grad_hidden, grad_context, sketch.reshape(1, piece * rank))


def solution(mesh):
    return jax.shard_map(
        on_device,
        mesh=mesh,
        in_specs=(
            P("dp", "tensor"),
            P(("dp", "tensor"), None),
            P("dp", "tensor"),
            P(),
            P(("dp", "tensor"), None),
            P(("dp", "tensor"), None),
            P("tensor", None),
            P(),
            P(("dp", "tensor")),
        ),
        out_specs=(P(("dp", "tensor"), None), P("dp", "tensor"), P("dp", "tensor")),
        check_vma=False,
    )
```

time: 288 us -> 158 us (0.55)
  waiting for transfers between devices: 168 us -> 0 us
  Pallas kernels: 0 us -> 147 us
  blocking collectives: 62.3 us -> 0 us
  matrix products: 33.7 us -> 0 us
  between operations: 15.8 us -> 0.64 us
  local copies, waits for them, and re-layouts: 2.79 us -> 9.96 us
  other arithmetic: 5.17 us -> 0 us
    pallas_call x0 -> x1, Pallas kernels: none -> 147 us  [on_device(): pl.pallas_call(functools.partial(kernel, dp, tp, group), out_shape=(jax.S...]
    all_gather x2 -> x0, waiting for transfers between devices: 123 us -> none  [the longest x1 123 us: on_device(): weight_full = lax.all_gather(out_weight, 'dp', axis=0, tiled=True)]
    unnamed x1 -> x0, blocking collectives: 62.3 us -> none
    reduce_scatter x2 -> x0, waiting for transfers between devices: 43.6 us -> none  [the longest x1 34.7 us: on_device(): lax.psum_scatter(lax.dot_general(context, weight_full, (((1,), (1,)), (()...]
    dot_general x5 -> x0, matrix products: 33.7 us -> none  [the longest x1 16.9 us: on_device(): lax.dot_general(context, weight_full, (((1,), (1,)), ((), ())), preferred...]
    unnamed x23 -> x6, local copies, waits for them, and re-layouts: 2.79 us -> 8.57 us
  transfers between devices with their start and end apart: 5 -> 0, of which waited for: 3 -> 0; matrix products, arithmetic and copies ran while one was open for 8% -> 0% of each run, Pallas kernels for 0% -> 0%
where the time goes in v1:
time: 158 us; the launch traced here: 157 us
  Pallas kernels  147 us (93%)
  local copies, waits for them, and re-layouts  9.96 us (6%)
    pallas_call x1, Pallas kernels, on_device(): pl.pallas_call(functools.partial(kernel, dp, tp, group), out_shape=(jax.S...  147 us
    unnamed x6, local copies, waits for them, and re-layouts  8.57 us

profile of v1, /device:TPU:0, one launch (start us, length us, event | category | flops | bytes accessed | tf_op | source)
XLA Modules:
  0.0 157.4 jit_solution(522184845385259168)
XLA Ops:
  0.6 2.1 %copy.12.in_hbm = s32[1536,64]{1,0:T(8,128)} copy(s32[1536,64]{0,1:T(8,128)} %param.15) | data formatting | bytes 786432 | tf_op args[6]
  2.8 3.0 %copy.13.out_hbm = s32[5120,64]{1,0:T(8,128)} copy(s32[5120,64]{0,1:T(8,128)} %param.16) | data formatting | bytes 2621440 | tf_op args[7]
  5.8 146.8 %shard_map.112 = (bf16[128,5120]{1,0:T(8,128)(2,1)}, bf16[256,1536]{1,0:T(8,128)(2,1)}, f32[32,64]{1,0:T(8,128)}) custom-call(bf16[256,1536]{1,0:T(8,128)(2,1)} %context_hbm.1, bf16[128,5120]{1,0:T(8,128)(2,1)} %residual_hbm.1, bf16[320,1536]{1,0:T(8,128)(2,1)} %weight_hbm.1, f32[1,5120]{1,0:T(1,128)} %bitcast.2, bf16[128,5120]{1,0:T(8,128)(2,1)} %normed_hbm.1, ...), custom_call_target="tpu_custom_call" | custom-call | flops 8053063680 | bytes 16777216 | tf_op jit(solution)/shard_map/pallas_call | solution.py:467
  152.6 1.4 reshape.17
  154.0 0.0 copy-start
  154.0 2.5 %copy.16 = bf16[128,5120]{1,0:T(8,128)(2,1)} copy(bf16[128,5120]{1,0:T(8,128)(2,1)} %get-tuple-element.12) | data formatting | bytes 2621440
  156.5 0.0 copy-done
  156.5 0.9 copy.17
Async XLA Ops:
  154.0 2.5 %copy-start = (bf16[256,1536]{1,0:T(8,128)(2,1)S(1)}, bf16[256,1536]{1,0:T(8,128)(2,1)}, u32[]{:S(2)}) copy-start(bf16[256,1536]{1,0:T(8,128)(2,1)} %get-tuple-element.13) | copy-start | bytes 2359300

commit v2 on v1

--- a/solution.py
+++ b/solution.py
@@ -114,50 +114,61 @@
     def index(a0, b0, c0):
         return (a0 * 2 + b0) * 2 + c0
 
-    def send_weight(i, way, to):
+    cut = shard // 32 * 16
+    halves = ((0, cut), (cut, shard - cut))
+
+    def send_weight(i, h, way, to):
+        first, count = halves[h]
+        where = pl.ds(pl.multiple_of(i * shard + first, 16), count)
         return pltpu.make_async_remote_copy(
-            src_ref=weight.at[place(i)],
-            dst_ref=weight.at[place(i)],
-            send_sem=w_send.at[way, i],
-            recv_sem=w_recv.at[i],
+            src_ref=weight.at[where],
+            dst_ref=weight.at[where],
+            send_sem=w_send.at[way, h, i],
+            recv_sem=w_recv.at[h, i],
             device_id=(to, t),
             device_id_type=MESH,
         )
 
-    def await_weight(i):
-        send_weight(i, 0, index(a, b, 1 - c)).wait_recv()
+    def await_weight(i, h):
+        send_weight(i, h, 0, index(a, b, 1 - c)).wait_recv()
 
     def peer(k):
         return lax.rem(t + 1 + k, tp)
 
-    def ways(a0, act):
-        i = index(a0, b, c)
-
-        @pl.when((a0 >= a) & (a > 0))
+    def crosses(a0, at, h):
+        far = lax.abs(at - a0) >= 2
+        end = (a0 == 0) | (a0 == lines - 1)
+        return jnp.logical_not(far & end) if h == 1 else jnp.bool_(True)
+
+    def ways(a0, column, h, act):
+        b0 = lax.rem(b + column, 2)
+        i = index(a0, b0, c)
+        along = column == 0
+
+        @pl.when((a0 >= a) & (a > 0) & (along | jnp.logical_not(crosses(a0, a - 1, h))))
         def _():
-            act(send_weight(i, 2, index(a - 1, b, c)))
-
-        @pl.when((a0 <= a) & (a < lines - 1))
+            act(send_weight(i, h, 2, index(a - 1, b, c)))
+
+        @pl.when(
+            (a0 <= a) & (a < lines - 1) & (along | jnp.logical_not(crosses(a0, a + 1, h)))
+        )
         def _():
-            act(send_weight(i, 3, index(a + 1, b, c)))
-
-        act(send_weight(i, 1, index(a, 1 - b, c)))
-        act(send_weight(i, 0, index(a, b, 1 - c)))
-
-    def pass_on(a0, column):
-        @pl.when(column == 0)
+            act(send_weight(i, h, 3, index(a + 1, b, c)))
+
+        @pl.when(along & crosses(a0, a, h))
         def _():
-            @pl.when(a0 != a)
-            def _():
-                await_weight(index(a0, b, c))
-
-            ways(a0, lambda copy: copy.start())
-
-        @pl.when(column == 1)
+            act(send_weight(i, h, 1, index(a, 1 - b, c)))
+
+        act(send_weight(i, h, 0, index(a, b, 1 - c)))
+
+    def pass_on(h, a0, column):
+        i = index(a0, lax.rem(b + column, 2), c)
+
+        @pl.when((a0 != a) | (column != 0))
         def _():
-            i = index(a0, 1 - b, c)
-            await_weight(i)
-            send_weight(i, 0, index(a, b, 1 - c)).start()
+            await_weight(i, h)
+
+        ways(a0, column, h, lambda copy: copy.start())
 
     def send_part(k, g):
         return pltpu.make_async_remote_copy(
@@ -228,7 +239,8 @@
 
     def whole_chip(a0, column):
         b0 = lax.rem(b + column, 2)
-        await_weight(index(a0, b0, 1 - c))
+        for h in (1, 0):
+            await_weight(index(a0, b0, 1 - c), h)
 
     def chip_forward(a0, column):
         whole_chip(a0, column)
@@ -241,7 +253,12 @@
         loads[1].wait()
         loads[2].wait()
         proj_all[...] = (
-            jnp.dot(context[...], in_table[...].astype(f32).astype(bf16), preferred_element_type=f32)
+            lax.dot_general(
+                context[...],
+                in_table[...].astype(f32).astype(bf16),
+                (((1,), (1,)), ((), ())),
+                preferred_element_type=f32,
+            )
             * in_scale
         ).astype(bf16)
         for k in range(tp - 1):
@@ -249,14 +266,17 @@
         for copy in loads[3:]:
             copy.wait()
 
-    pass_on(a, jnp.int32(0))
+    for h in (1, 0):
+        pass_on(h, a, jnp.int32(0))
     first_loads()
 
     @pl.loop(1, lines + 3)
     def _(s):
-        @pl.loop(0, 4)
-        def _(e):
-            event(e, s, pass_on)
+        for h in (1, 0):
+
+            @pl.loop(0, 4)
+            def _(e):
+                event(e, s, functools.partial(pass_on, h))
 
         if group == 2:
 
@@ -322,7 +342,12 @@
             send_gh(k, g).start()
 
     out_proj = (
-        jnp.dot(gh_out[...], out_table[...].astype(f32).astype(bf16), preferred_element_type=f32)
+        lax.dot_general(
+            gh_out[...],
+            out_table[...].astype(f32).astype(bf16),
+            (((1,), (1,)), ((), ())),
+            preferred_element_type=f32,
+        )
         * out_scale
     )
     in_proj = proj_all[own_rows, :].astype(f32)
@@ -419,9 +444,9 @@
 
     @pl.loop(0, lines)
     def _(a0):
-        ways(a0, lambda copy: copy.wait_send())
-        i = index(a0, 1 - b, c)
-        send_weight(i, 0, index(a, b, 1 - c)).wait_send()
+        for column in (0, 1):
+            for h in (1, 0):
+                ways(a0, jnp.int32(column), h, lambda copy: copy.wait_send())
 
     for k in range(tp - 1):
         send_proj(k).wait_send()
@@ -479,8 +504,8 @@
             pltpu.VMEM((rows, width), bf16),
             pltpu.VMEM((rows, width), bf16),
             pltpu.VMEM((rows, width), bf16),
-            pltpu.VMEM((heads, rank), jnp.int32),
-            pltpu.VMEM((width, rank), jnp.int32),
+            pltpu.VMEM((rank, heads), jnp.int32),
+            pltpu.VMEM((rank, width), jnp.int32),
             pltpu.VMEM((groups, tokens, cols), bf16),
             pltpu.VMEM((tp - 1, groups, rows, cols), bf16),
             pltpu.VMEM((groups, rows, cols), f32),
@@ -495,8 +520,8 @@
             pltpu.VMEM((dp, piece, rank), f32),
             pltpu.VMEM((dp, piece, rank), f32),
             dma((7,)),
-            dma((4, dp)),
-            dma((dp,)),
+            dma((4, 2, dp)),
+            dma((2, dp)),
             dma((tp - 1, groups)),
             dma((tp - 1, groups)),
             dma((tp - 1, groups)),
@@ -521,8 +546,8 @@
         norm_gain.reshape(1, width),
         normed_grad,
         stream_grad,
-        sketch_in,
-        sketch_out,
+        sketch_in.T,
+        sketch_out.T,
         example_ids.reshape(1, rows),
     )
     return (grad_hidden, grad_context, sketch.reshape(1, piece * rank))

time: 158 us -> 142 us (0.90)
  Pallas kernels: 147 us -> 136 us
  local copies, waits for them, and re-layouts: 9.96 us -> 4.81 us
    pallas_call x1, Pallas kernels: 147 us -> 136 us  [on_device(): pl.pallas_call(functools.partial(kernel, dp, tp, group), out_shape=(jax.S...]
    unnamed x6 -> x4, local copies, waits for them, and re-layouts: 8.57 us -> 3.41 us
where the time goes in v2:
time: 142 us
  Pallas kernels  136 us (96%)
  local copies, waits for them, and re-layouts  4.81 us (3%)
    pallas_call x1, Pallas kernels, on_device(): pl.pallas_call(functools.partial(kernel, dp, tp, group), out_shape=(jax.S...  136 us
    unnamed x4, local copies, waits for them, and re-layouts  3.41 us

profile of v2, /device:TPU:0, one launch (start us, length us, event | category | flops | bytes accessed | tf_op | source)
XLA Modules:
  0.0 141.7 jit_solution(14038282850514647773)
XLA Ops:
  0.6 136.2 %shard_map.112 = (bf16[128,5120]{1,0:T(8,128)(2,1)}, bf16[256,1536]{1,0:T(8,128)(2,1)}, f32[32,64]{1,0:T(8,128)}) custom-call(bf16[256,1536]{1,0:T(8,128)(2,1)} %context_hbm.1, bf16[128,5120]{1,0:T(8,128)(2,1)} %residual_hbm.1, bf16[320,1536]{1,0:T(8,128)(2,1)} %weight_hbm.1, f32[1,5120]{1,0:T(1,128)} %bitcast.6, bf16[128,5120]{1,0:T(8,128)(2,1)} %normed_hbm.1, ...), custom_call_target="tpu_custom_call" | custom-call | flops 8053063680 | bytes 16777216 | tf_op jit(solution)/shard_map/pallas_call | solution.py:492
  136.9 1.4 reshape.17
  138.3 0.0 copy-start
  138.3 2.5 %copy.14 = bf16[128,5120]{1,0:T(8,128)(2,1)} copy(bf16[128,5120]{1,0:T(8,128)(2,1)} %get-tuple-element.12) | data formatting | bytes 2621440
  140.8 0.0 copy-done
  140.8 0.9 copy.15
Async XLA Ops:
  138.3 2.5 %copy-start = (bf16[256,1536]{1,0:T(8,128)(2,1)S(1)}, bf16[256,1536]{1,0:T(8,128)(2,1)}, u32[]{:S(2)}) copy-start(bf16[256,1536]{1,0:T(8,128)(2,1)} %get-tuple-element.13) | copy-start | bytes 2359300

commit v3 on v2

--- a/solution.py
+++ b/solution.py
@@ -63,6 +63,16 @@
     skt_recv,
     skd_send,
     skd_recv,
+    early_stream,
+    early_normed,
+    early_hidden,
+    hidden_send,
+    stat_send,
+    stat_in,
+    early_sent,
+    early_recv,
+    stat_sent,
+    stat_recv,
 ):
     me = lax.axis_index("dp")
     t = lax.axis_index("tensor")
@@ -73,6 +83,7 @@
     shard = weight_hbm.shape[0]
     cols = group * shard
     groups = width // cols
+    early = group == 2 and tp > 1
     in_scale = 1.0 / math.sqrt(context.shape[1] * tp)
     out_scale = 1.0 / math.sqrt(width)
 
@@ -214,6 +225,43 @@
         square[...] += jnp.sum(value * value, axis=-1, keepdims=True)
         cross[...] += jnp.sum(value * weighted_of(g), axis=-1, keepdims=True)
 
+    def ship(n, k, j):
+        source = (
+            stream.at[:, block(2 * j + b)],
+            normed.at[:, block(2 * j + b)],
+            hidden_send.at[j],
+        )[n]
+        target = (early_stream, early_normed, early_hidden)[n]
+        return pltpu.make_async_remote_copy(
+            src_ref=source,
+            dst_ref=target.at[tp - 2 - k, j],
+            send_sem=early_sent.at[n, k, j],
+            recv_sem=early_recv.at[n, tp - 2 - k, j],
+            device_id=(me, peer(k)),
+            device_id_type=MESH,
+        )
+
+    def await_ship(n, k, j):
+        target = (early_stream, early_normed, early_hidden)[n]
+        pltpu.make_async_remote_copy(
+            src_ref=target.at[k, j],
+            dst_ref=target.at[k, j],
+            send_sem=early_sent.at[n, k, j],
+            recv_sem=early_recv.at[n, k, j],
+            device_id=(me, peer(k)),
+            device_id_type=MESH,
+        ).wait_recv()
+
+    def send_stat(k):
+        return pltpu.make_async_remote_copy(
+            src_ref=stat_send,
+            dst_ref=stat_in.at[tp - 2 - k],
+            send_sem=stat_sent.at[k],
+            recv_sem=stat_recv.at[tp - 2 - k],
+            device_id=(me, peer(k)),
+            device_id_type=MESH,
+        )
+
     square[...] = jnp.zeros_like(square)
     cross[...] = jnp.zeros_like(cross)
     loads[0].wait()
@@ -247,7 +295,15 @@
         forward(a0 * 2 + lax.rem(b + column, 2))
 
     def chip_stats(a0, column):
-        gather_stats(a0 * 2 + lax.rem(b + column, 2))
+        g = a0 * 2 + lax.rem(b + column, 2)
+        gather_stats(g)
+        if early:
+
+            @pl.when(column == 0)
+            def _():
+                hidden_send[a0] = hidden[g].astype(bf16)
+                for k in range(tp - 1):
+                    ship(2, k, a0).start()
 
     def first_loads():
         loads[1].wait()
@@ -265,6 +321,13 @@
             send_proj(k).start()
         for copy in loads[3:]:
             copy.wait()
+        if early:
+
+            @pl.loop(0, lines)
+            def _(j):
+                for k in range(tp - 1):
+                    ship(0, k, j).start()
+                    ship(1, k, j).start()
 
     for h in (1, 0):
         pass_on(h, a, jnp.int32(0))
@@ -308,6 +371,11 @@
     pull = rstd * rstd * rstd * (cross[...] * (1.0 / width))
     square[...] = rstd
     cross[...] = pull
+    if early:
+        lane = lax.broadcasted_iota(jnp.int32, (rows, 128), 1)
+        stat_send[...] = jnp.where(lane < 64, rstd, pull)
+        for k in range(tp - 1):
+            send_stat(k).start()
 
     def send_gh(k, g):
         return pltpu.make_async_remote_copy(
@@ -329,8 +397,7 @@
             device_id_type=MESH,
         ).wait_recv()
 
-    @pl.loop(0, groups)
-    def _(g):
+    def own_grad(g):
         value = (
             stream[:, block(g)].astype(f32)
             + square[...] * weighted_of(g)
@@ -338,8 +405,23 @@
         ).astype(bf16)
         gh_all[t, g] = value
         gh_out[:, block(g)] = value
+
+    def sent(act):
+        @pl.loop(0, lines if early else groups)
+        def _(j):
+            act(2 * j + 1 - b if early else j)
+
+    def own_and_send(g):
+        own_grad(g)
         for k in range(tp - 1):
             send_gh(k, g).start()
+
+    sent(own_and_send)
+    if early:
+
+        @pl.loop(0, lines)
+        def _(j):
+            own_grad(2 * j + b)
 
     out_proj = (
         lax.dot_general(
@@ -377,23 +459,19 @@
     for k in range(tp - 1):
         send_skt(k).start()
 
-    def backward(row, g0):
-        @pl.loop(0, groups)
-        def _(g):
-            g0(g)
-            product = jnp.dot(gh_all[row, g], weight[block(g), :], preferred_element_type=f32)
-
-            @pl.when(g == 0)
-            def _():
-                total[...] = product
-
-            @pl.when(g > 0)
-            def _():
-                total[...] += product
-
+    def add(row, g):
+        total[...] += jnp.dot(gh_all[row, g], weight[block(g), :], preferred_element_type=f32)
+
+    def finish(row):
         gc_out[pl.ds(pl.multiple_of(row * rows, rows), rows), :] = total[...].astype(bf16)
 
-    backward(t, lambda g: None)
+    total[...] = jnp.zeros_like(total)
+
+    @pl.loop(0, groups)
+    def _(g):
+        add(t, g)
+
+    finish(t)
 
     summed = sk_all[pl.ds(pl.multiple_of(t * piece, piece), piece), :]
     for k in range(tp - 1):
@@ -432,7 +510,28 @@
         send_skd(r).start()
 
     for k in range(tp - 1):
-        backward(peer(k), functools.partial(await_gh, k))
+        total[...] = jnp.zeros_like(total)
+        if early:
+            send_stat(tp - 2 - k).wait_recv()
+
+            @pl.loop(0, lines)
+            def _(j):
+                g = 2 * j + b
+                for n in range(3):
+                    await_ship(n, k, j)
+                gh_all[peer(k), g] = (
+                    early_stream[k, j].astype(f32)
+                    + stat_in[k, :, 0:1] * (gain_ref[:, block(g)] * early_normed[k, j].astype(f32))
+                    - early_hidden[k, j].astype(f32) * stat_in[k, :, 64:65]
+                ).astype(bf16)
+                add(peer(k), g)
+
+        def arrived(g):
+            await_gh(k, g)
+            add(peer(k), g)
+
+        sent(arrived)
+        finish(peer(k))
 
     sk_out[...] = jnp.where(owner == me, sk_out[...], 0.0)
 
@@ -455,7 +554,15 @@
         @pl.loop(0, groups)
         def _(g):
             send_part(k, g).wait_send()
-            send_gh(k, g).wait_send()
+
+        sent(lambda g: send_gh(k, g).wait_send())
+        if early:
+            send_stat(k).wait_send()
+
+            @pl.loop(0, lines)
+            def _(j):
+                for n in range(3):
+                    ship(n, k, j).wait_send()
 
     @pl.loop(1, dp)
     def _(k):
@@ -484,6 +591,7 @@
         group *= 2
     cols = group * shard
     groups = width // cols
+    early = (dp // 4, rows, cols) if group == 2 else (1, 16, 128)
     piece = rank // tp
     hbm = pl.BlockSpec(memory_space=pl.ANY)
     vmem = pl.BlockSpec(memory_space=pltpu.VMEM)
@@ -532,6 +640,16 @@
             dma((tp - 1,)),
             dma((dp,)),
             dma((dp,)),
+            pltpu.VMEM((tp - 1,) + early, bf16),
+            pltpu.VMEM((tp - 1,) + early, bf16),
+            pltpu.VMEM((tp - 1,) + early, bf16),
+            pltpu.VMEM(early, bf16),
+            pltpu.VMEM((rows, 128), f32),
+            pltpu.VMEM((tp - 1, rows, 128), f32),
+            dma((3, tp - 1, early[0])),
+            dma((3, tp - 1, early[0])),
+            dma((tp - 1,)),
+            dma((tp - 1,)),
         ],
         compiler_params=pltpu.CompilerParams(
             collective_id=0, has_side_effects=True, vmem_limit_bytes=56 * 1024 * 1024

time: 142 us -> 143 us (level)
  no operation moved by 1% of the time
where the time goes in v3:
time: 143 us; the launch traced here: 142 us
  Pallas kernels  137 us (96%)
  local copies, waits for them, and re-layouts  4.81 us (3%)
    pallas_call x1, Pallas kernels, on_device(): pl.pallas_call(functools.partial(kernel, dp, tp, group), out_shape=(jax.S...  137 us
    unnamed x4, local copies, waits for them, and re-layouts  3.41 us

profile of v3, /device:TPU:0, one launch (start us, length us, event | category | flops | bytes accessed | tf_op | source)
XLA Modules:
  0.0 142.5 jit_solution(2248955239094171882)
XLA Ops:
  0.6 137.0 %shard_map.112 = (bf16[128,5120]{1,0:T(8,128)(2,1)}, bf16[256,1536]{1,0:T(8,128)(2,1)}, f32[32,64]{1,0:T(8,128)}) custom-call(bf16[256,1536]{1,0:T(8,128)(2,1)} %context_hbm.1, bf16[128,5120]{1,0:T(8,128)(2,1)} %residual_hbm.1, bf16[320,1536]{1,0:T(8,128)(2,1)} %weight_hbm.1, f32[1,5120]{1,0:T(1,128)} %bitcast.6, bf16[128,5120]{1,0:T(8,128)(2,1)} %normed_hbm.1, ...), custom_call_target="tpu_custom_call" | custom-call | flops 8053063680 | bytes 16777216 | tf_op jit(solution)/shard_map/pallas_call | solution.py:600
  137.7 1.4 reshape.17
  139.1 0.0 copy-start
  139.1 2.5 %copy.14 = bf16[128,5120]{1,0:T(8,128)(2,1)} copy(bf16[128,5120]{1,0:T(8,128)(2,1)} %get-tuple-element.12) | data formatting | bytes 2621440
  141.6 0.0 copy-done
  141.6 0.9 copy.15
Async XLA Ops:
  139.1 2.5 %copy-start = (bf16[256,1536]{1,0:T(8,128)(2,1)S(1)}, bf16[256,1536]{1,0:T(8,128)(2,1)}, u32[]{:S(2)}) copy-start(bf16[256,1536]{1,0:T(8,128)(2,1)} %get-tuple-element.13) | copy-start | bytes 2359300

commit v4 on v3

--- a/solution.py
+++ b/solution.py
@@ -335,27 +335,27 @@
 
     @pl.loop(1, lines + 3)
     def _(s):
+        if group == 2:
+
+            @pl.loop(0, 4)
+            def _(e):
+                event(e, s - 1, chip_forward)
+
+            @pl.loop(0, 4)
+            def _(e):
+                event(e, s - 2, chip_stats)
+
+        else:
+
+            @pl.loop(0, 4)
+            def _(e):
+                event(e, s - 1, whole_chip)
+
         for h in (1, 0):
 
             @pl.loop(0, 4)
             def _(e):
                 event(e, s, functools.partial(pass_on, h))
-
-        if group == 2:
-
-            @pl.loop(0, 4)
-            def _(e):
-                event(e, s - 1, chip_forward)
-
-            @pl.loop(0, 4)
-            def _(e):
-                event(e, s - 2, chip_stats)
-
-        else:
-
-            @pl.loop(0, 4)
-            def _(e):
-                event(e, s - 1, whole_chip)
 
     if group != 2:
 

time: 143 us -> 130 us (0.909)
  Pallas kernels: 137 us -> 125 us
    pallas_call x1, Pallas kernels: 137 us -> 125 us  [on_device(): pl.pallas_call(functools.partial(kernel, dp, tp, group), out_shape=(jax.S...]
where the time goes in v4:
time: 130 us
  Pallas kernels  125 us (96%)
  local copies, waits for them, and re-layouts  4.81 us (4%)
    pallas_call x1, Pallas kernels, on_device(): pl.pallas_call(functools.partial(kernel, dp, tp, group), out_shape=(jax.S...  125 us
    unnamed x4, local copies, waits for them, and re-layouts  3.41 us

profile of v4, /device:TPU:0, one launch (start us, length us, event | category | flops | bytes accessed | tf_op | source)
XLA Modules:
  0.0 130.0 jit_solution(15643850791221296474)
XLA Ops:
  0.6 124.6 %shard_map.112 = (bf16[128,5120]{1,0:T(8,128)(2,1)}, bf16[256,1536]{1,0:T(8,128)(2,1)}, f32[32,64]{1,0:T(8,128)}) custom-call(bf16[256,1536]{1,0:T(8,128)(2,1)} %context_hbm.1, bf16[128,5120]{1,0:T(8,128)(2,1)} %residual_hbm.1, bf16[320,1536]{1,0:T(8,128)(2,1)} %weight_hbm.1, f32[1,5120]{1,0:T(1,128)} %bitcast.6, bf16[128,5120]{1,0:T(8,128)(2,1)} %normed_hbm.1, ...), custom_call_target="tpu_custom_call" | custom-call | flops 8053063680 | bytes 16777216 | tf_op jit(solution)/shard_map/pallas_call | solution.py:600
  125.2 1.4 %reshape.17 = f32[1,2048]{1,0:T(1,128)} reshape(f32[32,64]{1,0:T(8,128)} %get-tuple-element.8) | data formatting | bytes 16384 | tf_op jit(solution)/shard_map/reshape | solution.py:671
  126.6 0.0 copy-start
  126.6 2.5 %copy.14 = bf16[128,5120]{1,0:T(8,128)(2,1)} copy(bf16[128,5120]{1,0:T(8,128)(2,1)} %get-tuple-element.12) | data formatting | bytes 2621440
  129.2 0.0 copy-done
  129.2 0.9 copy.15
Async XLA Ops:
  126.6 2.5 %copy-start = (bf16[256,1536]{1,0:T(8,128)(2,1)S(1)}, bf16[256,1536]{1,0:T(8,128)(2,1)}, u32[]{:S(2)}) copy-start(bf16[256,1536]{1,0:T(8,128)(2,1)} %get-tuple-element.13) | copy-start | bytes 2359300
